TPU v7x, 32 devices: a whole 2x2x4 slice. The times are simulated.
32 devices in a mesh: row: 4 (over x, core), col: 8 (over z, y).
Axes of the slice: x: 2, y: 2, z: 4, core: 2. Of those that a mesh axis runs over, the one named last changes fastest.
Arguments:
- pair: bfloat16 [768, 768, 128], P('row', 'col'), may hold values from -6 to 6
- ln_gain: float32 [128], replicated, may hold values from 0.25 to 1.75
- w_query: bfloat16 [128, 128], replicated, may hold values from -46 to 46
- w_key: bfloat16 [128, 128], replicated, may hold values from -0.5 to 0.5
- w_value: bfloat16 [128, 128], replicated, may hold values from -0.5 to 0.5
- w_gate: bfloat16 [128, 128], replicated, may hold values from -0.5 to 0.5
- w_bias: bfloat16 [128, 4], replicated, may hold values from -0.5 to 0.5
- w_out: bfloat16 [128, 128], replicated, may hold values from -0.5 to 0.5
- valid_length: int32 [1], replicated, may hold values from 384 to 768
Outputs:
- update: bfloat16 [768, 768, 128], P('row', 'col')
Inputs may be any that keep to these rules, and one draw needn't show every extreme that they name: Tokens 0 to valid_length - 1 are real, the others are padding.
All inputs are finite; a program needn't handle non-finite values.
Results may differ from a plain program's by a relative error of at most 0.014.
The roundings to bfloat16 on the way count: a program that leaves them out, or rounds other values in their place, can miss the bound.
Values may be sent and summed in bfloat16 or wider, within the bound.
A program may use at most 384 MiB of HBM per device.

v0:
```python
import jax
import jax.numpy as jnp
from jax import lax
from jax.sharding import PartitionSpec as P

epsilon = 1e-05


def normalize(pair_rows, ln_gain):
    widened = pair_rows.astype(jnp.float32)
    average = jnp.mean(widened, -1, keepdims=True)
    centred = widened - average
    spread = jnp.mean(centred * centred, -1, keepdims=True)
    return (centred * lax.rsqrt(spread + epsilon) * ln_gain).astype(jnp.bfloat16)


def per_device(pair, ln_gain, w_query, w_key, w_value, w_gate, w_bias, w_out, valid_length):
    tile_rows, tile_cols, channels = pair.shape
    heads = w_bias.shape[1]
    width = w_query.shape[1]
    head_size = width // heads
    across = lax.axis_size("col")
    own_rows = tile_rows // across
    columns = tile_cols * across
    query_scale = head_size ** (-0.5)
    length = valid_length[0]
    normed = normalize(pair, ln_gain)
    bias_tile = jnp.einsum(
        "abc,ch->hab", normed, w_bias, preferred_element_type=jnp.float32
    ).astype(jnp.bfloat16)
    merged = jnp.concatenate([w_query, w_key, w_value, w_gate], axis=1)
    normed_rows = lax.all_to_all(normed, "col", split_axis=0, concat_axis=1, tiled=True)
    target_shape = normed_rows.shape[:2] + (width,)
    flattened = normed_rows.reshape(-1, channels)
    projected = jnp.dot(flattened, merged, preferred_element_type=jnp.float32)
    query = (projected[:, :width] * query_scale).astype(jnp.bfloat16).reshape(target_shape)
    key_proj = projected[:, width : 2 * width].astype(jnp.bfloat16).reshape(target_shape)
    value_proj = projected[:, 2 * width : 3 * width].astype(jnp.bfloat16).reshape(target_shape)
    project_gating = (
        jax.nn.sigmoid(projected[:, 3 * width :]).astype(jnp.bfloat16).reshape(target_shape)
    )
    query, key_proj, value_proj, gating = (query, key_proj, value_proj, project_gating)
    query_heads = query.reshape(own_rows, columns, heads, head_size)
    key_heads = key_proj.reshape(own_rows, columns, heads, head_size)
    value_heads = value_proj.reshape(own_rows, columns, heads, head_size)
    positions = jnp.arange(columns, dtype=jnp.int32)
    key_valid = positions < length
    first_row = lax.axis_index("row") * tile_rows + lax.axis_index("col") * own_rows
    row_valid = first_row + jnp.arange(own_rows, dtype=jnp.int32) < length
    bias_cols = lax.all_gather(bias_tile, "col", axis=2, tiled=True)
    portion = lax.all_gather(bias_cols, "row", axis=1, tiled=True)
    extent = portion.shape[1]
    scores = jnp.einsum(
        "ijhd,ikhd->ihjk", query_heads, key_heads, preferred_element_type=jnp.float32
    )
    scores = scores + portion.astype(jnp.float32)[None]
    scores = jnp.where(key_valid, scores, -1e30)
    highest = jnp.max(scores, -1, keepdims=True)
    exponent = jnp.exp(scores - highest)
    totals = jnp.sum(exponent, -1)
    weights = exponent.astype(jnp.bfloat16)
    blended = jnp.einsum(
        "ihjk,ikhd->ijhd", weights, value_heads, preferred_element_type=jnp.float32
    )
    blended = blended / jnp.transpose(totals, (0, 2, 1))[..., None]
    gated = (gating.astype(jnp.float32) * blended.reshape(own_rows, extent, width)).astype(
        jnp.bfloat16
    )
    update = jnp.dot(gated.reshape(-1, width), w_out, preferred_element_type=jnp.float32).reshape(
        own_rows, columns, channels
    )
    inside = row_valid[:, None] & key_valid[None, :]
    update = jnp.where(inside[..., None], update, 0.0).astype(jnp.bfloat16)
    return lax.all_to_all(update, "col", split_axis=1, concat_axis=0, tiled=True)


def solution(mesh):
    placed = (P("row", "col", None), P(), P(), P(), P(), P(), P(), P(), P())
    return jax.shard_map(
        per_device, mesh=mesh, in_specs=placed, out_specs=P("row", "col", None), check_vma=False
    )
```

profile of v0, /device:TPU:0, one launch (start us, length us, event | category | flops | bytes accessed | tf_op | source)
XLA Modules:
  0.0 650.4 jit_solution(1903052083637613479)
XLA Ops:
  6.5 4.3 convert_reduce_fusion
  10.8 7.6 %fusion.8 = f32[192,96]{1,0:T(8,128)S(1)} fusion(bf16[192,96,128]{2,1,0:T(8,128)(2,1)} %param.9, f32[192,96]{1,0:T(8,128)S(1)} %broadcast_multiply_fusion), kind=kLoop, calls=%fused_computation.11 | loop fusion | flops 9418752 | bytes 4866048 | tf_op jit(solution)/shard_map/reduce_sum | solution.py:13
  18.5 6.6 %fusion.10 = bf16[192,96,128]{2,1,0:T(8,128)(2,1)} fusion(bf16[192,96,128]{2,1,0:T(8,128)(2,1)S(1)} %copy-done.1, f32[128]{0:T(128)S(1)} %copy-done.8, f32[192,96]{1,0:T(8,128)S(1)} %add_rsqrt_fusion, f32[192,96]{1,0:T(8,128)S(1)} %broadcast_multiply_fusion), kind=kLoop, calls=%fused_computation.13 | loop fusion | flops 11796480 | bytes 9585152 | tf_op jit(solution)/shard_map/convert_element_type | solution.py:14
  25.1 7.3 %all-to-all-start = ((bf16[192,96,128]{2,1,0:T(8,128)(2,1)}), bf16[192,96,128]{2,1,0:T(8,128)(2,1)}, u32[]{:S(2)}, u32[]{:S(2)}) async-start(bf16[192,96,128]{2,1,0:T(8,128)(2,1)} %fusion.10), calls=%async_computation | async-start | bytes 9437184 | tf_op jit(solution)/shard_map/all_to_all | solution.py:32
  32.5 5.3 fusion.24
  37.8 0.9 copy.61
  40.6 97.9 %all-gather.3.cloned.1.call-done = bf16[4,192,768]{1,0,2:T(4,128)(2,1)} async-done(((bf16[4,192,96]{1,0,2:T(4,128)(2,1)}), bf16[4,192,768]{1,0,2:T(4,128)(2,1)}) %all-gather.3.cloned.1.call-update) | async-done | bytes 1179664 | tf_op jit(solution)/shard_map/all_gather | solution.py:50
  138.5 4.1 copy.62
  142.6 13.2 %all-to-all-done = bf16[192,96,128]{2,1,0:T(8,128)(2,1)} async-done(((bf16[192,96,128]{2,1,0:T(8,128)(2,1)}), bf16[192,96,128]{2,1,0:T(8,128)(2,1)}, u32[]{:S(2)}, u32[]{:S(2)}) %all-to-all-start) | async-done | bytes 4718624 | tf_op jit(solution)/shard_map/all_to_all | solution.py:32
  155.9 5.9 copy.55
  161.8 23.0 %fusion.38 = (bf16[18432,512]{1,0:T(8,128)(2,1)}, f32[18432,512]{1,0:T(8,128)}) fusion(bf16[18432,128]{1,0:T(8,128)(2,1)} %bitcast.49, bf16[128,128]{1,0:T(8,128)(2,1)S(1)} %copy-done.3, bf16[128,128]{1,0:T(8,128)(2,1)S(1)} %copy-done.4, bf16[128,128]{1,0:T(8,128)(2,1)S(1)} %copy-done.5, bf16[128,128]{1,0:T(8,128)(2,1)S(1)} %copy-done.6), kind=kOutput, calls=%fused_computation.49 | convolution fusion | flops 2425880576 | bytes 61472768 | tf_op jit(solution)/shard_map/dot_general | solution.py:35
  184.8 8.3 %fusion.37 = (bf16[18432,128]{1,0:T(8,128)(2,1)}, bf16[18432,128]{1,0:T(8,128)(2,1)}) fusion(bf16[18432,512]{1,0:T(8,128)(2,1)} %get-tuple-element.7), kind=kLoop, calls=%fused_computation.48 | loop fusion | bytes 18874368 | tf_op jit(solution)/shard_map/slice | solution.py:38
  193.1 6.6 %copy.58 = bf16[18432,128]{0,1:T(8,128)(2,1)} copy(bf16[18432,128]{1,0:T(8,128)(2,1)} %get-tuple-element.6) | data formatting | bytes 9437184 | tf_op jit(solution)/shard_map/slice | solution.py:37
  199.7 5.7 copy.74
  205.5 6.7 %fusion.11 = bf16[18432,128]{1,0:T(8,128)(2,1)} fusion(f32[18432,512]{1,0:T(8,128)} %get-tuple-element.8), kind=kLoop, calls=%fused_computation.15 | loop fusion | flops 4718592 | bytes 14155776 | tf_op jit(solution)/shard_map/convert_element_type | solution.py:36
  212.2 6.6 %copy.57 = bf16[18432,128]{0,1:T(8,128)(2,1)} copy(bf16[18432,128]{1,0:T(8,128)(2,1)} %fusion.11) | data formatting | bytes 9437184 | tf_op jit(solution)/shard_map/convert_element_type | solution.py:36
  218.8 5.8 copy.73
  224.6 6.6 %copy.56 = bf16[18432,128]{0,1:T(8,128)(2,1)} copy(bf16[18432,128]{1,0:T(8,128)(2,1)} %get-tuple-element.5) | data formatting | bytes 9437184 | tf_op jit(solution)/shard_map/slice | solution.py:38
  231.2 5.7 copy.72
  236.9 6.8 %copy_convert_fusion = f32[4,768,768]{2,1,0:T(8,128)} fusion(bf16[4,768,768]{2,0,1:T(4,128)(2,1)} %all-gather.5.cloned.1.call-done), kind=kLoop, calls=%fused_computation.25 | loop fusion | flops 2359296 | bytes 14155776 | tf_op jit(solution)/shard_map/convert_element_type | solution.py:56
  243.7 9.6 %copy.64 = f32[4,768,768]{1,2,0:T(8,128)} copy(f32[4,768,768]{2,1,0:T(8,128)} %copy_convert_fusion) | data formatting | bytes 18874368 | tf_op jit(solution)/shard_map/convert_element_type | solution.py:56
  253.3 81.1 %fusion = (f32[24,4,768]{2,1,0:T(4,128)S(1)}, f32[24,4,768,768]{2,3,1,0:T(8,128)}) fusion(f32[4,768,768]{1,2,0:T(8,128)} %copy.64, pred[768]{0:T(1024)(128)(4,1)S(1)} %iota_compare_fusion, bf16[24,768,4,32]{1,0,3,2:T(8,128)(2,1)} %bitcast.50, bf16[24,768,4,32]{1,0,3,2:T(8,128)(2,1)} %bitcast.51), kind=kOutput, calls=%fused_computation.2 | convolution fusion | flops 3793674240 | bytes 245662464 | tf_op jit(solution)/shard_map/ijhd,ikhd->ihjk/dot_general | solution.py:53
  334.4 77.4 %fusion.1 = f32[24,4,768]{2,1,0:T(4,128)S(1)} fusion(f32[24,4,768,768]{2,3,1,0:T(8,128)} %get-tuple-element.10, f32[24,4,768]{2,1,0:T(4,128)S(1)} %get-tuple-element.9, f32[4,768,768]{1,2,0:T(8,128)} %copy.64, pred[768]{0:T(1024)(128)(4,1)S(1)} %iota_compare_fusion), kind=kLoop, calls=%fused_computation.3 | loop fusion | flops 226418688 | bytes 236520192 | tf_op jit(solution)/shard_map/reduce_sum | solution.py:60
  411.8 80.3 %bitcast_divide_fusion = f32[24,768,4,32]{1,3,2,0:T(8,128)} fusion(f32[24,4,768,768]{2,3,1,0:T(8,128)} %get-tuple-element.10, f32[24,4,768]{2,1,0:T(4,128)S(1)} %get-tuple-element.9, f32[4,768,768]{1,2,0:T(8,128)} %copy.64, pred[768]{0:T(1024)(128)(4,1)S(1)} %iota_compare_fusion, bf16[24,768,4,32]{1,0,3,2:T(8,128)(2,1)} %bitcast.52, ...), kind=kOutput, calls=%fused_computation.20 | convolution fusion | flops 3852730368 | bytes 250675968 | tf_op jit(solution)/shard_map/ihjk,ikhd->ijhd/dot_general | solution.py:62
  492.1 9.1 %copy.67 = f32[24,768,4,32]{1,0,3,2:T(8,128)S(1)} copy(f32[24,768,4,32]{1,3,2,0:T(8,128)} %bitcast_divide_fusion) | data formatting | bytes 18874368 | tf_op jit(solution)/shard_map/div | solution.py:65
  501.2 6.6 %copy.75 = f32[16,8,24,768]{3,1,2,0:T(8,128)} copy(f32[16,8,24,768]{3,2,1,0:T(8,128)S(1)} %bitcast.46) | data formatting | bytes 18874368
  507.8 9.6 %copy.68 = f32[18432,128]{1,0:T(8,128)} copy(f32[18432,128]{0,1:T(8,128)} %bitcast.47) | data formatting | bytes 18874368 | tf_op jit(solution)/shard_map/reshape | solution.py:66
  517.5 7.5 %multiply_convert_fusion = bf16[18432,128]{1,0:T(8,128)(2,1)S(1)} fusion(f32[18432,128]{1,0:T(8,128)} %copy.68, f32[18432,512]{1,0:T(8,128)} %get-tuple-element.8), kind=kLoop, calls=%fused_computation.22 | loop fusion | flops 16515072 | bytes 23592960 | tf_op jit(solution)/shard_map/convert_element_type | solution.py:66
  525.0 4.0 select_convert_fusion
  529.1 3.0 copy.69
  532.1 108.1 %all_to_all.33 = bf16[24,768,128]{2,0,1:T(8,128)(2,1)S(1)} all-to-all(bf16[24,768,128]{2,0,1:T(8,128)(2,1)S(1)} %copy.69), channel_id=1, replica_groups=mesh['row'=4,'col'=8] {'col'}, dimensions={1} | all-to-all | bytes 9437184 | tf_op jit(solution)/shard_map/all_to_all | solution.py:74
  640.2 3.1 copy.70
  (28 shorter events, 1.4 us)
Async XLA Ops:
  6.5 518.5 %copy-start = (bf16[128,128]{1,0:T(8,128)(2,1)S(1)}, bf16[128,128]{1,0:T(8,128)(2,1)}, u32[]{:S(2)}) copy-start(bf16[128,128]{1,0:T(8,128)(2,1)} %param.16) | copy-start | bytes 98308
  6.5 12.0 %copy-start.1 = (bf16[192,96,128]{2,1,0:T(8,128)(2,1)S(1)}, bf16[192,96,128]{2,1,0:T(8,128)(2,1)}, u32[]{:S(2)}) copy-start(bf16[192,96,128]{2,1,0:T(8,128)(2,1)} %param.9) | copy-start | bytes 14155780
  6.5 12.0 %copy-start.8 = (f32[128]{0:T(128)S(1)}, f32[128]{0:T(128)}, u32[]{:S(2)}) copy-start(f32[128]{0:T(128)} %param.10) | copy-start | bytes 1540
  18.5 14.0 %copy-start.7 = (bf16[128,4]{0,1:T(4,128)(2,1)S(1)}, bf16[128,4]{0,1:T(4,128)(2,1)}, u32[]{:S(2)}) copy-start(bf16[128,4]{0,1:T(4,128)(2,1)} %param.15) | copy-start | bytes 3076
  25.1 130.8 %all-to-all-start = ((bf16[192,96,128]{2,1,0:T(8,128)(2,1)}), bf16[192,96,128]{2,1,0:T(8,128)(2,1)}, u32[]{:S(2)}, u32[]{:S(2)}) async-start(bf16[192,96,128]{2,1,0:T(8,128)(2,1)} %fusion.10), calls=%async_computation | async-start | bytes 9437184 | tf_op jit(solution)/shard_map/all_to_all | solution.py:32
  32.4 129.4 %copy-start.3 = (bf16[128,128]{1,0:T(8,128)(2,1)S(1)}, bf16[128,128]{1,0:T(8,128)(2,1)}, u32[]{:S(2)}) copy-start(bf16[128,128]{1,0:T(8,128)(2,1)} %param.14) | copy-start | bytes 98308
  32.4 129.4 %copy-start.4 = (bf16[128,128]{1,0:T(8,128)(2,1)S(1)}, bf16[128,128]{1,0:T(8,128)(2,1)}, u32[]{:S(2)}) copy-start(bf16[128,128]{1,0:T(8,128)(2,1)} %param.13) | copy-start | bytes 98308
  32.4 129.4 %copy-start.5 = (bf16[128,128]{1,0:T(8,128)(2,1)S(1)}, bf16[128,128]{1,0:T(8,128)(2,1)}, u32[]{:S(2)}) copy-start(bf16[128,128]{1,0:T(8,128)(2,1)} %param.12) | copy-start | bytes 98308
  32.4 129.4 %copy-start.6 = (bf16[128,128]{1,0:T(8,128)(2,1)S(1)}, bf16[128,128]{1,0:T(8,128)(2,1)}, u32[]{:S(2)}) copy-start(bf16[128,128]{1,0:T(8,128)(2,1)} %param.11) | copy-start | bytes 98308
  32.5 106.1 %all-gather.3.cloned.1.call-start = ((), (), s32[]{:S(2)}) async-start(), calls=%async_computation.2 | async-start | bytes 1769472 | tf_op jit(solution)/shard_map/all_gather | solution.py:50
  38.7 198.2 %all-gather.5.cloned.1.call-start = ((), (), s32[]{:S(2)}) async-start(), calls=%async_computation.3 | async-start | bytes 5898240 | tf_op jit(solution)/shard_map/all_gather | solution.py:51
  517.5 7.6 %copy-start.2 = (pred[24,768]{1,0:T(8,128)(4,1)S(1)}, pred[24,768]{1,0:T(8,128)(4,1)}, u32[]{:S(2)}) copy-start(pred[24,768]{1,0:T(8,128)(4,1)} %broadcast_and_fusion) | copy-start | bytes 55300
Sparse Core Ops, SparseCore 0:
  38.8 99.6 all-gather.2
  142.8 35.5 all-gather.4
where the time goes:
time: 656 us; the launch traced here: 650 us
  matrix products  194 us (30%)
  other arithmetic  118 us (18%)
  waiting for transfers between devices  111 us (17%)
  blocking collectives  108 us (16%)
  local copies, waits for them, and re-layouts  97.4 us (15%)
  between operations  14.5 us (2%)
  starting transfers between devices  7.89 us (1%)
    all_to_all x1, blocking collectives, per_device(): lax.all_to_all(update, 'col', split_axis=1, concat_axis=0, tiled=True)  108 us
    all_gather x1, waiting for transfers between devices, per_device(): bias_cols = lax.all_gather(bias_tile, 'col', axis=2, tiled=True)  97.9 us
    dot_general x1, matrix products, per_device(): jnp.einsum('ijhd,ikhd->ihjk', query_heads, key_heads, preferred_element_t...  81.1 us
    dot_general x1, matrix products, per_device(): jnp.einsum('ihjk,ikhd->ijhd', weights, value_heads, preferred_element_typ...  80.3 us
    reduce_sum x1, other arithmetic, per_device(): totals = jnp.sum(exponent, -1)  77.4 us
    unnamed x22, local copies, waits for them, and re-layouts  23.9 us
    dot_general x1, matrix products, per_device(): projected = jnp.dot(flattened, merged, preferred_element_type=jnp.float32)  23 us
    slice x2, local copies, waits for them, and re-layouts, per_device(): projected[:, 2 * width:3 * width].astype(jnp.bfloat16).reshape(target_shape)  14.9 us
  transfers between devices with their start and end apart: 3, of which 2 were waited for; matrix products, arithmetic and copies ran while one was open for 14% of the time, Pallas kernels for 0%

commit v1 on v0

v1 whole, which is shorter than its diff:
```python
import functools

import jax
import jax.numpy as jnp
from jax import lax
from jax.experimental import pallas as pl
from jax.experimental.pallas import tpu as pltpu
from jax.sharding import PartitionSpec as P

epsilon = 1e-05
CHUNKS = 3


def normalize(pair_rows, ln_gain):
    widened = pair_rows.astype(jnp.float32)
    average = jnp.mean(widened, -1, keepdims=True)
    centred = widened - average
    spread = jnp.mean(centred * centred, -1, keepdims=True)
    return (centred * lax.rsqrt(spread + epsilon) * ln_gain).astype(jnp.bfloat16)


def attend(heads, block, normed_ref, bias_ref, merged_ref, out_w_ref, update_ref):
    across, _, tile_cols, channels = normed_ref.shape
    columns, width = across * tile_cols, out_w_ref.shape[0]
    head_size = width // heads
    normed = normed_ref[...].reshape(columns, channels)
    scale = head_size ** (-0.5)

    def project(part):
        weight = merged_ref[:, part * width : (part + 1) * width]
        return jnp.dot(normed, weight, preferred_element_type=jnp.float32)

    query = (project(0) * scale).astype(jnp.bfloat16)
    key_proj = project(1).astype(jnp.bfloat16)
    value_proj = project(2).astype(jnp.bfloat16)
    gating = jax.nn.sigmoid(project(3)).astype(jnp.bfloat16).astype(jnp.float32)
    summed = jnp.concatenate([value_proj, jnp.ones_like(value_proj)], axis=1)
    lane_head = lax.broadcasted_iota(jnp.int32, (block, width), 1) // head_size
    updates = []
    for start in range(0, columns, block):
        span = slice(start, start + block)
        blended = jnp.zeros((block, width), jnp.float32)
        for head in range(heads):
            mine = lane_head == head
            picked = jnp.where(mine, query[span], jnp.zeros((), jnp.bfloat16))
            scores = lax.dot_general(
                picked, key_proj, (((1,), (1,)), ((), ())), preferred_element_type=jnp.float32
            )
            scores = scores + bias_ref[head, span, :].astype(jnp.float32)
            highest = jnp.max(scores, -1, keepdims=True)
            weights = jnp.exp(scores - highest).astype(jnp.bfloat16)
            both = jnp.dot(weights, summed, preferred_element_type=jnp.float32)
            blended = jnp.where(mine, both[:, :width] / both[:, width:], blended)
        gated = (gating[span] * blended).astype(jnp.bfloat16)
        update = jnp.dot(gated, out_w_ref[...], preferred_element_type=jnp.float32)
        updates.append(update.astype(jnp.bfloat16))
    update_ref[...] = jnp.concatenate(updates, axis=0).reshape(update_ref.shape)


def block_of(columns):
    for block in (256, 128, 64, 32, 16):
        if columns % block == 0:
            return block
    return columns


def attention(normed_rows, bias, merged, w_out):
    across, rows, tile_cols, channels = normed_rows.shape
    columns = across * tile_cols
    piece = pl.BlockSpec((across, 1, tile_cols, channels), lambda i: (0, i, 0, 0))
    heads, width = bias.shape[0], w_out.shape[0]
    whole = lambda i: (0, 0)
    cells = rows * heads * columns * columns
    return pl.pallas_call(
        functools.partial(attend, heads, block_of(columns)),
        grid=(rows,),
        in_specs=[
            piece,
            pl.BlockSpec(bias.shape, lambda i: (0, 0, 0)),
            pl.BlockSpec(merged.shape, whole),
            pl.BlockSpec(w_out.shape, whole),
        ],
        out_specs=piece,
        out_shape=jax.ShapeDtypeStruct(normed_rows.shape, jnp.bfloat16),
        compiler_params=pltpu.CompilerParams(vmem_limit_bytes=48 * 1024 * 1024),
        cost_estimate=pl.CostEstimate(
            flops=cells * 768, bytes_accessed=8 * cells // columns * 64, transcendentals=cells
        ),
    )(normed_rows, bias, merged, w_out)


def per_device(pair, ln_gain, w_query, w_key, w_value, w_gate, w_bias, w_out, valid_length):
    tile_rows, tile_cols, channels = pair.shape
    across = lax.axis_size("col")
    own_rows = tile_rows // across
    length = valid_length[0]
    row_at = lax.axis_index("row") * tile_rows + jnp.arange(tile_rows, dtype=jnp.int32)
    col_at = lax.axis_index("col") * tile_cols + jnp.arange(tile_cols, dtype=jnp.int32)
    normed = normalize(pair, ln_gain)
    bias_tile = jnp.einsum(
        "abc,ch->hab", normed, w_bias, preferred_element_type=jnp.float32
    )
    bias_tile = jnp.where(col_at < length, bias_tile, -1e30).astype(jnp.bfloat16)
    merged = jnp.concatenate([w_query, w_key, w_value, w_gate], axis=1)
    bias_cols = lax.all_gather(bias_tile, "col", axis=2, tiled=True)
    bias = lax.all_gather(bias_cols, "row", axis=1, tiled=True)
    step = own_rows // CHUNKS if own_rows % CHUNKS == 0 else own_rows
    tiles = normed.reshape(across, own_rows, tile_cols, channels)
    pieces = []
    for first in range(0, own_rows, step):
        part = lax.all_to_all(tiles[:, first : first + step], "col", split_axis=0, concat_axis=0)
        update = attention(part, bias, merged, w_out)
        pieces.append(lax.all_to_all(update, "col", split_axis=0, concat_axis=0))
    update = jnp.concatenate(pieces, axis=1).reshape(tile_rows, tile_cols, channels)
    inside = (row_at < length)[:, None] & (col_at < length)[None, :]
    return jnp.where(inside[..., None], update, jnp.zeros((), jnp.bfloat16))


def solution(mesh):
    placed = (P("row", "col", None), P(), P(), P(), P(), P(), P(), P(), P())
    return jax.shard_map(
        per_device, mesh=mesh, in_specs=placed, out_specs=P("row", "col", None), check_vma=False
    )
```

time: 656 us -> 360 us (0.55)
  matrix products: 194 us -> 5.27 us
  Pallas kernels: 0 us -> 116 us
  other arithmetic: 118 us -> 26.9 us
  local copies, waits for them, and re-layouts: 97.4 us -> 12.8 us
  waiting for transfers between devices: 111 us -> 82 us
  blocking collectives: 108 us -> 80.5 us
  starting transfers between devices: 7.89 us -> 21.5 us
    dot_general x4 -> x0, matrix products: 189 us -> none  [the longest x1 81.1 us: per_device(): jnp.einsum('ijhd,ikhd->ihjk', query_heads, key_heads, preferred_element_t...]
    pallas_call x0 -> x3, Pallas kernels: none -> 116 us  [attention(): pl.pallas_call(functools.partial(attend, heads, block_of(columns)), grid=...]
    reduce_sum x1 -> x0, other arithmetic: 77.4 us -> none  [per_device(): totals = jnp.sum(exponent, -1)]
    all_gather x1, waiting for transfers between devices: 97.9 us -> 47 us  [per_device(): bias_cols = lax.all_gather(bias_tile, 'col', axis=2, tiled=True)]
    all_to_all x1 -> x2, blocking collectives: 108 us -> 80.5 us  [per_device(): lax.all_to_all(tiles[:, first:first + step], 'col', split_axis=0, concat_...]
    all_to_all x1 -> x4, waiting for transfers between devices: 13.2 us -> 34.9 us  [the longest x3 34.9 us: per_device(): pieces.append(lax.all_to_all(update, 'col', split_axis=0, concat_axis=0))]
    convert_element_type x3 -> x0, other arithmetic: 21 us -> none  [the longest x1 7.54 us: per_device(): (gating.astype(jnp.float32) * blended.reshape(own_rows, extent, width)).a...]
    unnamed x22 -> x25, local copies, waits for them, and re-layouts: 23.9 us -> 3.85 us
  transfers between devices with their start and end apart: 3 -> 6, of which waited for: 2 -> 2; matrix products, arithmetic and copies ran while one was open for 14% -> 1% of each run, Pallas kernels for 0% -> 32%
where the time goes in v1:
time: 360 us
  Pallas kernels  116 us (32%)
  waiting for transfers between devices  82 us (23%)
  blocking collectives  80.5 us (22%)
  other arithmetic  26.9 us (7%)
  starting transfers between devices  21.5 us (6%)
  between operations  14.3 us (4%)
  local copies, waits for them, and re-layouts  12.8 us (4%)
  matrix products  5.27 us (1%)
    pallas_call x3, Pallas kernels, attention(): pl.pallas_call(functools.partial(attend, heads, block_of(columns)), grid=...  116 us
    all_to_all x2, blocking collectives, per_device(): lax.all_to_all(tiles[:, first:first + step], 'col', split_axis=0, concat_...  80.5 us
    all_gather x1, waiting for transfers between devices, per_device(): bias_cols = lax.all_gather(bias_tile, 'col', axis=2, tiled=True)  47 us
    all_to_all x3, waiting for transfers between devices, per_device(): pieces.append(lax.all_to_all(update, 'col', split_axis=0, concat_axis=0))  34.9 us
    all_to_all x3, starting transfers between devices, per_device(): pieces.append(lax.all_to_all(update, 'col', split_axis=0, concat_axis=0))  17.9 us
    convert_element_type x1, other arithmetic, normalize(): (centred * lax.rsqrt(spread + epsilon) * ln_gain).astype(jnp.bfloat16)  7.63 us
  transfers between devices with their start and end apart: 6, of which 2 were waited for; matrix products, arithmetic and copies ran while one was open for 1% of the time, Pallas kernels for 32%

profile of v1, /device:TPU:0, one launch (start us, length us, event | category | flops | bytes accessed | tf_op | source)
XLA Modules:
  0.0 359.6 jit_solution(11292149027573028672)
XLA Ops:
  6.5 4.3 %convert_reduce_fusion = f32[192,96]{1,0:T(8,128)S(1)} fusion(bf16[192,96,128]{2,1,0:T(8,128)(2,1)} %param.9), kind=kLoop, calls=%fused_computation.1 | loop fusion | flops 4700160 | bytes 4792320 | tf_op jit(solution)/shard_map/reduce_sum | solution.py:16
  10.8 6.3 %fusion.2 = f32[192,96]{1,0:T(8,128)S(1)} fusion(bf16[192,96,128]{2,1,0:T(8,128)(2,1)S(1)} %copy-done.5, f32[192,96]{1,0:T(8,128)S(1)} %broadcast_multiply_fusion), kind=kLoop, calls=%fused_computation.4 | loop fusion | flops 9418752 | bytes 4866048 | tf_op jit(solution)/shard_map/reduce_sum | solution.py:18
  17.9 7.6 %fusion.4 = bf16[192,96,128]{2,1,0:T(8,128)(2,1)} fusion(bf16[192,96,128]{2,1,0:T(8,128)(2,1)} %param.9, f32[128]{0:T(128)S(1)} %copy-done.10, f32[192,96]{1,0:T(8,128)S(1)} %add_rsqrt_fusion, f32[192,96]{1,0:T(8,128)S(1)} %broadcast_multiply_fusion), kind=kLoop, calls=%fused_computation.6 | loop fusion | flops 11796480 | bytes 9585152 | tf_op jit(solution)/shard_map/convert_element_type | solution.py:19
  25.5 5.3 %fusion.6 = bf16[4,192,96]{2,0,1:T(4,128)(2,1)S(1)} fusion(bf16[192,96,128]{2,1,0:T(8,128)(2,1)} %fusion.4, pred[96]{0:T(512)(128)(4,1)S(1)} %add_compare_fusion.1, bf16[128,4]{0,1:T(4,128)(2,1)S(1)} %copy-done), kind=kOutput, calls=%fused_computation.11 | convolution fusion | flops 19021824 | bytes 4867168 | tf_op jit(solution)/shard_map/abc,ch->hab/dot_general | solution.py:100
  30.8 0.9 copy.11
  31.7 0.0 all-gather.3.cloned.1.call-update
  31.7 0.0 all-gather.5.cloned.1.call-start
  31.7 47.0 %all-gather.3.cloned.1.call-done = bf16[4,192,768]{1,0,2:T(4,128)(2,1)} async-done(((bf16[4,192,96]{1,0,2:T(4,128)(2,1)}), bf16[4,192,768]{1,0,2:T(4,128)(2,1)}) %all-gather.3.cloned.1.call-update) | async-done | bytes 1179664 | tf_op jit(solution)/shard_map/all_gather | solution.py:105
  78.7 3.6 %copy.12 = bf16[4,192,768]{2,1,0:T(8,128)(2,1)} copy(bf16[4,192,768]{1,0,2:T(4,128)(2,1)} %all-gather.3.cloned.1.call-done) | data formatting | bytes 2359296 | tf_op jit(solution)/shard_map/all_gather | solution.py:105
  82.3 0.0 all-gather.5.cloned.1.call-update
  82.4 4.5 %fusion.8 = (bf16[8,8,96,128]{3,2,1,0:T(8,128)(2,1)}, bf16[8,8,96,128]{3,2,1,0:T(8,128)(2,1)S(1)}, bf16[8,8,96,128]{3,2,1,0:T(8,128)(2,1)S(1)}) fusion(bf16[8,24,96,128]{3,2,1,0:T(8,128)(2,1)} %bitcast.12), kind=kLoop, calls=%fused_computation.22 | loop fusion | bytes 9437184 | tf_op jit(solution)/shard_map/slice | solution.py:111
  86.9 0.0 copy-start.4
  86.9 40.5 %all_to_all.30.normed_ref = bf16[8,8,96,128]{3,2,1,0:T(8,128)(2,1)} all-to-all(bf16[8,8,96,128]{3,2,1,0:T(8,128)(2,1)S(1)} %get-tuple-element.6), channel_id=1, replica_groups=mesh['row'=4,'col'=8] {'col'}, dimensions={0} | all-to-all | bytes 3145728 | tf_op jit(solution)/shard_map/all_to_all | solution.py:111
  127.3 40.1 %all_to_all.31.normed_ref = bf16[8,8,96,128]{3,2,1,0:T(8,128)(2,1)S(1)} all-to-all(bf16[8,8,96,128]{3,2,1,0:T(8,128)(2,1)S(1)} %get-tuple-element.7), channel_id=1, replica_groups=mesh['row'=4,'col'=8] {'col'}, dimensions={0} | all-to-all | bytes 3145728 | tf_op jit(solution)/shard_map/all_to_all | solution.py:111
  167.4 3.6 all-to-all-start
  171.1 0.0 all-gather.5.cloned.1.call-done.bias_ref
  171.2 1.4 copy-done.1
  172.6 38.6 %shard_map.93 = bf16[8,8,96,128]{3,2,1,0:T(8,128)(2,1)S(1)} custom-call(bf16[8,8,96,128]{3,2,1,0:T(8,128)(2,1)S(1)} %copy-done.1, bf16[4,768,768]{2,1,0:T(8,128)(2,1)} %all-gather.5.cloned.1.call-done.bias_ref, bf16[128,512]{1,0:T(8,128)(2,1)S(1)} %constant_dynamic-update-slice_fusion.merged_ref, bf16[128,128]{1,0:T(8,128)(2,1)S(1)} %copy-done.4), custom_call_target="tpu_custom_call" | custom-call | flops 14495514624 | bytes 12582912 | tf_op jit(solution)/shard_map/pallas_call | solution.py:74
  211.1 0.0 copy-start.3
  211.1 1.1 copy-done.3
  212.3 0.0 all-to-all-done.normed_ref
  212.3 6.0 %all-to-all-start.5 = ((bf16[8,8,96,128]{3,2,1,0:T(8,128)(2,1)}), bf16[8,8,96,128]{3,2,1,0:T(8,128)(2,1)}, u32[]{:S(2)}, u32[]{:S(2)}) async-start(bf16[8,8,96,128]{3,2,1,0:T(8,128)(2,1)} %copy-done.3), calls=%async_computation.5 | async-start | bytes 3145728 | tf_op jit(solution)/shard_map/all_to_all | solution.py:113
  218.2 38.6 %shard_map.92 = bf16[8,8,96,128]{3,2,1,0:T(8,128)(2,1)S(1)} custom-call(bf16[8,8,96,128]{3,2,1,0:T(8,128)(2,1)S(1)} %all_to_all.31.normed_ref, bf16[4,768,768]{2,1,0:T(8,128)(2,1)} %all-gather.5.cloned.1.call-done.bias_ref, bf16[128,512]{1,0:T(8,128)(2,1)S(1)} %constant_dynamic-update-slice_fusion.merged_ref, bf16[128,128]{1,0:T(8,128)(2,1)S(1)} %copy-done.4), custom_call_target="tpu_custom_call" | custom-call | flops 14495514624 | bytes 12582912 | tf_op jit(solution)/shard_map/pallas_call | solution.py:74
  256.8 1.2 copy-done.2
  258.1 0.0 all-to-all-done.5
  258.1 6.0 %all-to-all-start.3 = ((bf16[8,8,96,128]{3,2,1,0:T(8,128)(2,1)}), bf16[8,8,96,128]{3,2,1,0:T(8,128)(2,1)}, u32[]{:S(2)}, u32[]{:S(2)}) async-start(bf16[8,8,96,128]{3,2,1,0:T(8,128)(2,1)} %copy-done.2), calls=%async_computation.3 | async-start | bytes 3145728 | tf_op jit(solution)/shard_map/all_to_all | solution.py:113
  264.1 39.2 %shard_map.91 = bf16[8,8,96,128]{3,2,1,0:T(8,128)(2,1)} custom-call(bf16[8,8,96,128]{3,2,1,0:T(8,128)(2,1)S(1)} %all-to-all-done.normed_ref, bf16[4,768,768]{2,1,0:T(8,128)(2,1)} %all-gather.5.cloned.1.call-done.bias_ref, bf16[128,512]{1,0:T(8,128)(2,1)S(1)} %constant_dynamic-update-slice_fusion.merged_ref, bf16[128,128]{1,0:T(8,128)(2,1)S(1)} %copy-done.4), custom_call_target="tpu_custom_call" | custom-call | flops 14495514624 | bytes 12582912 | tf_op jit(solution)/shard_map/pallas_call | solution.py:74
  303.2 6.0 %all-to-all-start.1 = ((bf16[8,8,96,128]{3,2,1,0:T(8,128)(2,1)}), bf16[8,8,96,128]{3,2,1,0:T(8,128)(2,1)S(1)}, u32[]{:S(2)}, u32[]{:S(2)}) async-start(bf16[8,8,96,128]{3,2,1,0:T(8,128)(2,1)} %shard_map.91), calls=%async_computation.1 | async-start | bytes 3145728 | tf_op jit(solution)/shard_map/all_to_all | solution.py:113
  309.2 0.1 broadcast_and_fusion
  309.3 34.9 %all-to-all-done.1 = bf16[8,8,96,128]{3,2,1,0:T(8,128)(2,1)S(1)} async-done(((bf16[8,8,96,128]{3,2,1,0:T(8,128)(2,1)}), bf16[8,8,96,128]{3,2,1,0:T(8,128)(2,1)S(1)}, u32[]{:S(2)}, u32[]{:S(2)}) %all-to-all-start.1) | async-done | bytes 1572896 | tf_op jit(solution)/shard_map/all_to_all | solution.py:113
  344.3 2.1 pad_maximum_fusion
  346.4 6.4 %bitcast_select_fusion = bf16[192,96,128]{2,1,0:T(8,128)(2,1)} fusion(bf16[8,24,96,128]{3,2,1,0:T(8,128)(2,1)S(1)} %pad_maximum_fusion, pred[192,96]{1,0:T(8,128)(4,1)S(1)} %broadcast_and_fusion), kind=kLoop, calls=%fused_computation.8 | loop fusion | flops 2359296 | bytes 9455616 | tf_op jit(solution)/shard_map/jit(_where)/select_n | solution.py:116
  (27 shorter events, 0.1 us)
Async XLA Ops:
  6.5 19.0 %copy-start = (bf16[128,4]{0,1:T(4,128)(2,1)S(1)}, bf16[128,4]{0,1:T(4,128)(2,1)}, u32[]{:S(2)}) copy-start(bf16[128,4]{0,1:T(4,128)(2,1)} %param.15) | copy-start | bytes 3076
  6.5 72.2 %all-gather.3.cloned.1.call-start = ((), (), s32[]{:S(2)}) async-start(), calls=%async_computation.6 | async-start | bytes 1769472 | tf_op jit(solution)/shard_map/all_gather | solution.py:105
  6.5 4.3 %copy-start.5 = (bf16[192,96,128]{2,1,0:T(8,128)(2,1)S(1)}, bf16[192,96,128]{2,1,0:T(8,128)(2,1)}, u32[]{:S(2)}) copy-start(bf16[192,96,128]{2,1,0:T(8,128)(2,1)} %param.9) | copy-start | bytes 14155780
  6.5 11.3 %copy-start.10 = (f32[128]{0:T(128)S(1)}, f32[128]{0:T(128)}, u32[]{:S(2)}) copy-start(f32[128]{0:T(128)} %param.10) | copy-start | bytes 1540
  31.7 139.4 %all-gather.5.cloned.1.call-start = ((), (), s32[]{:S(2)}) async-start(), calls=%async_computation.7 | async-start | bytes 5898240 | tf_op jit(solution)/shard_map/all_gather | solution.py:106
  86.8 84.2 %copy-start.6 = (bf16[128,128]{1,0:T(8,128)(2,1)S(1)}, bf16[128,128]{1,0:T(8,128)(2,1)}, u32[]{:S(2)}) copy-start(bf16[128,128]{1,0:T(8,128)(2,1)} %param.11) | copy-start | bytes 98308
  86.8 84.2 %copy-start.7 = (bf16[128,128]{1,0:T(8,128)(2,1)S(1)}, bf16[128,128]{1,0:T(8,128)(2,1)}, u32[]{:S(2)}) copy-start(bf16[128,128]{1,0:T(8,128)(2,1)} %param.12) | copy-start | bytes 98308
  86.8 84.2 %copy-start.8 = (bf16[128,128]{1,0:T(8,128)(2,1)S(1)}, bf16[128,128]{1,0:T(8,128)(2,1)}, u32[]{:S(2)}) copy-start(bf16[128,128]{1,0:T(8,128)(2,1)} %param.13) | copy-start | bytes 98308
  86.8 84.2 %copy-start.9 = (bf16[128,128]{1,0:T(8,128)(2,1)S(1)}, bf16[128,128]{1,0:T(8,128)(2,1)}, u32[]{:S(2)}) copy-start(bf16[128,128]{1,0:T(8,128)(2,1)} %param.14) | copy-start | bytes 98308
  86.9 84.3 %copy-start.4 = (bf16[128,128]{1,0:T(8,128)(2,1)S(1)}, bf16[128,128]{1,0:T(8,128)(2,1)}, u32[]{:S(2)}) copy-start(bf16[128,128]{1,0:T(8,128)(2,1)} %out_w_ref.5) | copy-start | bytes 98308
  167.4 44.9 %all-to-all-start = ((bf16[8,8,96,128]{3,2,1,0:T(8,128)(2,1)}), bf16[8,8,96,128]{3,2,1,0:T(8,128)(2,1)S(1)}, u32[]{:S(2)}, u32[]{:S(2)}) async-start(bf16[8,8,96,128]{3,2,1,0:T(8,128)(2,1)} %get-tuple-element.5), calls=%async_computation | async-start | bytes 3145728 | tf_op jit(solution)/shard_map/all_to_all | solution.py:111
  171.1 1.4 copy-start.1
  211.1 1.1 copy-start.3
  212.3 45.8 %all-to-all-start.5 = ((bf16[8,8,96,128]{3,2,1,0:T(8,128)(2,1)}), bf16[8,8,96,128]{3,2,1,0:T(8,128)(2,1)}, u32[]{:S(2)}, u32[]{:S(2)}) async-start(bf16[8,8,96,128]{3,2,1,0:T(8,128)(2,1)} %copy-done.3), calls=%async_computation.5 | async-start | bytes 3145728 | tf_op jit(solution)/shard_map/all_to_all | solution.py:113
  256.8 1.3 copy-start.2
  258.1 45.1 %all-to-all-start.3 = ((bf16[8,8,96,128]{3,2,1,0:T(8,128)(2,1)}), bf16[8,8,96,128]{3,2,1,0:T(8,128)(2,1)}, u32[]{:S(2)}, u32[]{:S(2)}) async-start(bf16[8,8,96,128]{3,2,1,0:T(8,128)(2,1)} %copy-done.2), calls=%async_computation.3 | async-start | bytes 3145728 | tf_op jit(solution)/shard_map/all_to_all | solution.py:113
  303.2 41.0 %all-to-all-start.1 = ((bf16[8,8,96,128]{3,2,1,0:T(8,128)(2,1)}), bf16[8,8,96,128]{3,2,1,0:T(8,128)(2,1)S(1)}, u32[]{:S(2)}, u32[]{:S(2)}) async-start(bf16[8,8,96,128]{3,2,1,0:T(8,128)(2,1)} %shard_map.91), calls=%async_computation.1 | async-start | bytes 3145728 | tf_op jit(solution)/shard_map/all_to_all | solution.py:113
Sparse Core Ops, SparseCore 0:
  31.8 46.8 all-gather.2
  82.5 36.2 all-gather.4

commit v2 on v1

--- a/solution.py
+++ b/solution.py
@@ -8,18 +8,47 @@
 from jax.sharding import PartitionSpec as P
 
 epsilon = 1e-05
-CHUNKS = 3
+CHUNKS = 2
 
 
-def normalize(pair_rows, ln_gain):
-    widened = pair_rows.astype(jnp.float32)
+def prepare(pair_ref, gain_ref, bias_w_ref, normed_ref, bias_ref):
+    widened = pair_ref[...].astype(jnp.float32)
     average = jnp.mean(widened, -1, keepdims=True)
     centred = widened - average
     spread = jnp.mean(centred * centred, -1, keepdims=True)
-    return (centred * lax.rsqrt(spread + epsilon) * ln_gain).astype(jnp.bfloat16)
+    normed = (centred * lax.rsqrt(spread + epsilon) * gain_ref[...]).astype(jnp.bfloat16)
+    normed_ref[...] = normed
+    bias_ref[...] = lax.dot_general(
+        bias_w_ref[...], normed, (((1,), (1,)), ((), ())), preferred_element_type=jnp.float32
+    )
 
 
-def attend(heads, block, normed_ref, bias_ref, merged_ref, out_w_ref, update_ref):
+def normalize(pair, ln_gain, w_bias):
+    tile_rows, tile_cols, channels = pair.shape
+    cells, heads = tile_rows * tile_cols, w_bias.shape[1]
+    block = next(n for n in (2304, 768, 256, 128, cells) if cells % n == 0)
+    normed, bias = pl.pallas_call(
+        prepare,
+        grid=(cells // block,),
+        in_specs=[
+            pl.BlockSpec((block, channels), lambda i: (i, 0)),
+            pl.BlockSpec((1, channels), lambda i: (0, 0)),
+            pl.BlockSpec((heads, channels), lambda i: (0, 0)),
+        ],
+        out_specs=[
+            pl.BlockSpec((block, channels), lambda i: (i, 0)),
+            pl.BlockSpec((heads, block), lambda i: (0, i)),
+        ],
+        out_shape=[
+            jax.ShapeDtypeStruct((cells, channels), jnp.bfloat16),
+            jax.ShapeDtypeStruct((heads, cells), jnp.float32),
+        ],
+        compiler_params=pltpu.CompilerParams(vmem_limit_bytes=32 * 1024 * 1024),
+    )(pair.reshape(cells, channels), ln_gain.reshape(1, channels), w_bias.T)
+    return normed, bias.reshape(heads, tile_rows, tile_cols)
+
+
+def attend(heads, block, limits_ref, normed_ref, bias_ref, merged_ref, out_w_ref, update_ref):
     across, _, tile_cols, channels = normed_ref.shape
     columns, width = across * tile_cols, out_w_ref.shape[0]
     head_size = width // heads
@@ -36,6 +65,9 @@
     gating = jax.nn.sigmoid(project(3)).astype(jnp.bfloat16).astype(jnp.float32)
     summed = jnp.concatenate([value_proj, jnp.ones_like(value_proj)], axis=1)
     lane_head = lax.broadcasted_iota(jnp.int32, (block, width), 1) // head_size
+    length, first_row = limits_ref[0], limits_ref[1]
+    limit = jnp.where(first_row + pl.program_id(0) < length, length, 0)
+    place = lax.broadcasted_iota(jnp.int32, (block, channels), 0)
     updates = []
     for start in range(0, columns, block):
         span = slice(start, start + block)
@@ -53,6 +85,7 @@
             blended = jnp.where(mine, both[:, :width] / both[:, width:], blended)
         gated = (gating[span] * blended).astype(jnp.bfloat16)
         update = jnp.dot(gated, out_w_ref[...], preferred_element_type=jnp.float32)
+        update = jnp.where(place + start < limit, update, 0.0)
         updates.append(update.astype(jnp.bfloat16))
     update_ref[...] = jnp.concatenate(updates, axis=0).reshape(update_ref.shape)
 
@@ -64,7 +97,7 @@
     return columns
 
 
-def attention(normed_rows, bias, merged, w_out):
+def attention(limits, normed_rows, bias, merged, w_out):
     across, rows, tile_cols, channels = normed_rows.shape
     columns = across * tile_cols
     piece = pl.BlockSpec((across, 1, tile_cols, channels), lambda i: (0, i, 0, 0))
@@ -75,6 +108,7 @@
         functools.partial(attend, heads, block_of(columns)),
         grid=(rows,),
         in_specs=[
+            pl.BlockSpec(memory_space=pltpu.SMEM),
             piece,
             pl.BlockSpec(bias.shape, lambda i: (0, 0, 0)),
             pl.BlockSpec(merged.shape, whole),
@@ -86,7 +120,7 @@
         cost_estimate=pl.CostEstimate(
             flops=cells * 768, bytes_accessed=8 * cells // columns * 64, transcendentals=cells
         ),
-    )(normed_rows, bias, merged, w_out)
+    )(limits, normed_rows, bias, merged, w_out)
 
 
 def per_device(pair, ln_gain, w_query, w_key, w_value, w_gate, w_bias, w_out, valid_length):
@@ -94,26 +128,26 @@
     across = lax.axis_size("col")
     own_rows = tile_rows // across
     length = valid_length[0]
-    row_at = lax.axis_index("row") * tile_rows + jnp.arange(tile_rows, dtype=jnp.int32)
+    first_own = lax.axis_index("row") * tile_rows + lax.axis_index("col") * own_rows
     col_at = lax.axis_index("col") * tile_cols + jnp.arange(tile_cols, dtype=jnp.int32)
-    normed = normalize(pair, ln_gain)
-    bias_tile = jnp.einsum(
-        "abc,ch->hab", normed, w_bias, preferred_element_type=jnp.float32
-    )
+    normed, bias_tile = normalize(pair, ln_gain, w_bias)
     bias_tile = jnp.where(col_at < length, bias_tile, -1e30).astype(jnp.bfloat16)
     merged = jnp.concatenate([w_query, w_key, w_value, w_gate], axis=1)
-    bias_cols = lax.all_gather(bias_tile, "col", axis=2, tiled=True)
+    heads = bias_tile.shape[0]
+    repeated = jnp.broadcast_to(bias_tile.reshape(1, -1, channels), (across, bias_tile.size // channels, channels))
+    bias_cols = lax.all_to_all(repeated, "col", split_axis=0, concat_axis=0)
+    bias_cols = bias_cols.reshape(across, heads, tile_rows, tile_cols)
+    bias_cols = jnp.moveaxis(bias_cols, 0, 2).reshape(heads, tile_rows, across * tile_cols)
     bias = lax.all_gather(bias_cols, "row", axis=1, tiled=True)
     step = own_rows // CHUNKS if own_rows % CHUNKS == 0 else own_rows
     tiles = normed.reshape(across, own_rows, tile_cols, channels)
     pieces = []
     for first in range(0, own_rows, step):
         part = lax.all_to_all(tiles[:, first : first + step], "col", split_axis=0, concat_axis=0)
-        update = attention(part, bias, merged, w_out)
+        limits = jnp.stack([length, first_own + first])
+        update = attention(limits, part, bias, merged, w_out)
         pieces.append(lax.all_to_all(update, "col", split_axis=0, concat_axis=0))
-    update = jnp.concatenate(pieces, axis=1).reshape(tile_rows, tile_cols, channels)
-    inside = (row_at < length)[:, None] & (col_at < length)[None, :]
-    return jnp.where(inside[..., None], update, jnp.zeros((), jnp.bfloat16))
+    return jnp.concatenate(pieces, axis=1).reshape(tile_rows, tile_cols, channels)
 
 
 def solution(mesh):

time: 360 us -> 321 us (0.89)
  waiting for transfers between devices: 82 us -> 0.04 us
  blocking collectives: 80.5 us -> 151 us
  other arithmetic: 26.9 us -> 4.47 us
  starting transfers between devices: 21.5 us -> 9.69 us
  local copies, waits for them, and re-layouts: 12.8 us -> 20 us
  matrix products: 5.27 us -> 0 us
  Pallas kernels: 116 us -> 120 us
    all_to_all x0 -> x2, blocking collectives: none -> 94.3 us  [the longest x1 58.3 us: per_device(): pieces.append(lax.all_to_all(update, 'col', split_axis=0, concat_axis=0))]
    all_gather x1 -> x0, waiting for transfers between devices: 47 us -> none  [per_device(): bias_cols = lax.all_gather(bias_tile, 'col', axis=2, tiled=True)]
    all_to_all x3 -> x1, waiting for transfers between devices: 34.9 us -> 0.01 us  [per_device(): pieces.append(lax.all_to_all(update, 'col', split_axis=0, concat_axis=0))]
    all_to_all x2 -> x1, blocking collectives: 80.5 us -> 56.9 us  [per_device(): lax.all_to_all(tiles[:, first:first + step], 'col', split_axis=0, concat_...]
    all_to_all x3 -> x1, starting transfers between devices: 17.9 us -> 5.93 us  [per_device(): pieces.append(lax.all_to_all(update, 'col', split_axis=0, concat_axis=0))]
    reduce_sum x2 -> x0, other arithmetic: 10.6 us -> none  [the longest x1 6.32 us: normalize(): spread = jnp.mean(centred * centred, -1, keepdims=True)]
    convert_element_type x1, other arithmetic: 7.63 us -> 0.05 us  [per_device(): jnp.where(col_at < length, bias_tile, -1e+30).astype(jnp.bfloat16)]
    pallas_call x0 -> x1, Pallas kernels: none -> 6.63 us  [normalize(): pl.pallas_call(prepare, grid=(cells // block,), in_specs=[pl.BlockSpec((b...]
  transfers between devices with their start and end apart: 6 -> 3, of which waited for: 2 -> 0; matrix products, arithmetic and copies ran while one was open for 1% -> 2% of each run, Pallas kernels for 32% -> 36%
where the time goes in v2:
time: 321 us; the launch traced here: 320 us
  blocking collectives  151 us (47%)
  Pallas kernels  120 us (37%)
  local copies, waits for them, and re-layouts  20 us (6%)
  between operations  14.2 us (4%)
  starting transfers between devices  9.69 us (3%)
  other arithmetic  4.47 us (1%)
    pallas_call x2, Pallas kernels, attention(): pl.pallas_call(functools.partial(attend, heads, block_of(columns)), grid=...  114 us
    all_to_all x1, blocking collectives, per_device(): pieces.append(lax.all_to_all(update, 'col', split_axis=0, concat_axis=0))  58.3 us
    all_to_all x1, blocking collectives, per_device(): lax.all_to_all(tiles[:, first:first + step], 'col', split_axis=0, concat_...  56.9 us
    all_to_all x1, blocking collectives, per_device(): bias_cols = lax.all_to_all(repeated, 'col', split_axis=0, concat_axis=0)  36 us
    unnamed x27, local copies, waits for them, and re-layouts  10.5 us
    pallas_call x1, Pallas kernels, normalize(): pl.pallas_call(prepare, grid=(cells // block,), in_specs=[pl.BlockSpec((b...  6.63 us
  transfers between devices with their start and end apart: 3, of which 0 were waited for; matrix products, arithmetic and copies ran while one was open for 2% of the time, Pallas kernels for 36%

profile of v2, /device:TPU:0, one launch (start us, length us, event | category | flops | bytes accessed | tf_op | source)
XLA Modules:
  0.0 319.9 jit_solution(4273642772361393083)
XLA Ops:
  7.2 0.3 broadcast_in_dim.16
  7.5 0.0 copy-start.1
  7.5 2.3 copy-done.1
  9.9 0.7 copy-done.5
  10.6 0.7 copy-done.6
  11.2 6.6 %shard_map.91 = (bf16[18432,128]{1,0:T(8,128)(2,1)S(1)}, f32[4,18432]{1,0:T(4,128)S(1)}) custom-call(bf16[18432,128]{1,0:T(8,128)(2,1)S(1)} %bitcast.13, f32[1,128]{1,0:T(1,128)S(1)} %bitcast.15, bf16[4,128]{1,0:T(4,128)(2,1)S(1)} %bitcast.14), custom_call_target="tpu_custom_call" | custom-call | tf_op jit(solution)/shard_map/pallas_call | solution.py:30
  17.8 2.2 copy-done
  20.0 0.2 reshape.37
  20.2 0.1 select_convert_fusion
  20.3 0.2 broadcast_in_dim.18
  20.4 36.0 %all_to_all.25 = bf16[8,576,128]{2,1,0:T(8,128)(2,1)S(1)} all-to-all(bf16[8,576,128]{2,1,0:T(8,128)(2,1)S(1)} %broadcast_in_dim.18), channel_id=1, replica_groups=mesh['row'=4,'col'=8] {'col'}, dimensions={0} | all-to-all | bytes 2359296 | tf_op jit(solution)/shard_map/all_to_all | solution.py:138
  56.5 1.0 reshape.38
  57.5 1.0 copy.10
  58.5 2.2 reshape.39
  60.7 0.0 all-gather.2.cloned.1.call-update
  60.7 4.7 %fusion = (bf16[8,12,96,128]{3,2,1,0:T(8,128)(2,1)S(1)}, bf16[8,12,96,128]{3,2,1,0:T(8,128)(2,1)}) fusion(bf16[8,24,96,128]{3,2,1,0:T(8,128)(2,1)} %bitcast.12), kind=kLoop, calls=%fused_computation.9 | loop fusion | bytes 9437184 | tf_op jit(solution)/shard_map/slice | solution.py:146
  65.4 56.9 %all_to_all.26.normed_ref = bf16[8,12,96,128]{3,2,1,0:T(8,128)(2,1)} all-to-all(bf16[8,12,96,128]{3,2,1,0:T(8,128)(2,1)S(1)} %get-tuple-element.9), channel_id=1, replica_groups=mesh['row'=4,'col'=8] {'col'}, dimensions={0} | all-to-all | bytes 4718592 | tf_op jit(solution)/shard_map/all_to_all | solution.py:146
  122.3 0.0 copy-start.7
  122.3 3.8 %all-to-all-start.3 = ((bf16[8,12,96,128]{3,2,1,0:T(8,128)(2,1)}), bf16[8,12,96,128]{3,2,1,0:T(8,128)(2,1)S(1)}, u32[]{:S(2)}, u32[]{:S(2)}) async-start(bf16[8,12,96,128]{3,2,1,0:T(8,128)(2,1)} %get-tuple-element.10), calls=%async_computation.3 | async-start | bytes 4718592 | tf_op jit(solution)/shard_map/all_to_all | solution.py:146
  126.1 0.1 pad_add_fusion.limits_ref
  126.3 0.0 all-gather.2.cloned.1.call-done.bias_ref
  126.3 1.7 copy-done.2
  128.0 56.8 %shard_map.92 = bf16[8,12,96,128]{3,2,1,0:T(8,128)(2,1)S(1)} custom-call(s32[2]{0:T(128)S(1)} %pad_add_fusion.limits_ref, bf16[8,12,96,128]{3,2,1,0:T(8,128)(2,1)S(1)} %copy-done.2, bf16[4,768,768]{2,1,0:T(8,128)(2,1)} %all-gather.2.cloned.1.call-done.bias_ref, bf16[128,512]{1,0:T(8,128)(2,1)S(1)} %constant_dynamic-update-slice_fusion.merged_ref, ...), custom_call_target="tpu_custom_call" | custom-call | flops 21743271936 | bytes 18874368 | tf_op jit(solution)/shard_map/pallas_call | solution.py:107
  184.8 1.5 copy-done.3
  186.3 0.0 all-to-all-done.3.normed_ref
  186.3 5.9 %all-to-all-start.2 = ((bf16[8,12,96,128]{3,2,1,0:T(8,128)(2,1)}), bf16[8,12,96,128]{3,2,1,0:T(8,128)(2,1)}, u32[]{:S(2)}, u32[]{:S(2)}) async-start(bf16[8,12,96,128]{3,2,1,0:T(8,128)(2,1)} %copy-done.3), calls=%async_computation.2 | async-start | bytes 4718592 | tf_op jit(solution)/shard_map/all_to_all | solution.py:149
  192.2 0.1 pad_add_fusion.1.limits_ref
  192.3 56.8 %shard_map.93 = bf16[8,12,96,128]{3,2,1,0:T(8,128)(2,1)S(1)} custom-call(s32[2]{0:T(128)S(1)} %pad_add_fusion.1.limits_ref, bf16[8,12,96,128]{3,2,1,0:T(8,128)(2,1)S(1)} %all-to-all-done.3.normed_ref, bf16[4,768,768]{2,1,0:T(8,128)(2,1)} %all-gather.2.cloned.1.call-done.bias_ref, bf16[128,512]{1,0:T(8,128)(2,1)S(1)} %constant_dynamic-update-slice_fusion.merged_ref, ...), custom_call_target="tpu_custom_call" | custom-call | flops 21743271936 | bytes 18874368 | tf_op jit(solution)/shard_map/pallas_call | solution.py:107
  249.1 0.0 copy-start.4
  249.1 1.4 copy-done.4
  250.5 58.3 %all_to_all.27 = bf16[8,12,96,128]{3,2,1,0:T(8,128)(2,1)S(1)} all-to-all(bf16[8,12,96,128]{3,2,1,0:T(8,128)(2,1)} %copy-done.4), channel_id=1, replica_groups=mesh['row'=4,'col'=8] {'col'}, dimensions={0} | all-to-all | bytes 4718592 | tf_op jit(solution)/shard_map/all_to_all | solution.py:149
  308.8 4.3 %pad_maximum_fusion = bf16[8,24,96,128]{3,2,1,0:T(8,128)(2,1)} fusion(bf16[8,12,96,128]{3,2,1,0:T(8,128)(2,1)S(1)} %all_to_all.27, bf16[8,12,96,128]{3,2,1,0:T(8,128)(2,1)} %all-to-all-done.2), kind=kLoop, calls=%fused_computation | loop fusion | flops 2359296 | bytes 9437184 | tf_op jit(solution)/shard_map/concatenate | solution.py:150
  (22 shorter events, 0.1 us)
Async XLA Ops:
  6.5 119.8 %all-gather.2.cloned.1.call-start = ((), (), s32[]{:S(2)}) async-start(), calls=%async_computation.5 | async-start | bytes 5898240 | tf_op jit(solution)/shard_map/all_gather | solution.py:141
  7.5 2.3 copy-start.1
  9.9 0.7 copy-start.5
  10.6 0.7 copy-start.6
  17.8 2.2 copy-start
  122.3 3.9 %copy-start.8 = (bf16[128,128]{1,0:T(8,128)(2,1)S(1)}, bf16[128,128]{1,0:T(8,128)(2,1)}, u32[]{:S(2)}) copy-start(bf16[128,128]{1,0:T(8,128)(2,1)} %param.11) | copy-start | bytes 98308
  122.3 3.9 %copy-start.9 = (bf16[128,128]{1,0:T(8,128)(2,1)S(1)}, bf16[128,128]{1,0:T(8,128)(2,1)}, u32[]{:S(2)}) copy-start(bf16[128,128]{1,0:T(8,128)(2,1)} %param.12) | copy-start | bytes 98308
  122.3 3.9 %copy-start.10 = (bf16[128,128]{1,0:T(8,128)(2,1)S(1)}, bf16[128,128]{1,0:T(8,128)(2,1)}, u32[]{:S(2)}) copy-start(bf16[128,128]{1,0:T(8,128)(2,1)} %param.13) | copy-start | bytes 98308
  122.3 3.9 %copy-start.11 = (bf16[128,128]{1,0:T(8,128)(2,1)S(1)}, bf16[128,128]{1,0:T(8,128)(2,1)}, u32[]{:S(2)}) copy-start(bf16[128,128]{1,0:T(8,128)(2,1)} %param.14) | copy-start | bytes 98308
  122.3 4.0 %copy-start.7 = (bf16[128,128]{1,0:T(8,128)(2,1)S(1)}, bf16[128,128]{1,0:T(8,128)(2,1)}, u32[]{:S(2)}) copy-start(bf16[128,128]{1,0:T(8,128)(2,1)} %out_w_ref.3) | copy-start | bytes 98308
  122.3 64.0 %all-to-all-start.3 = ((bf16[8,12,96,128]{3,2,1,0:T(8,128)(2,1)}), bf16[8,12,96,128]{3,2,1,0:T(8,128)(2,1)S(1)}, u32[]{:S(2)}, u32[]{:S(2)}) async-start(bf16[8,12,96,128]{3,2,1,0:T(8,128)(2,1)} %get-tuple-element.10), calls=%async_computation.3 | async-start | bytes 4718592 | tf_op jit(solution)/shard_map/all_to_all | solution.py:146
  126.3 1.7 copy-start.2
  184.8 1.5 copy-start.3
  186.3 64.2 %all-to-all-start.2 = ((bf16[8,12,96,128]{3,2,1,0:T(8,128)(2,1)}), bf16[8,12,96,128]{3,2,1,0:T(8,128)(2,1)}, u32[]{:S(2)}, u32[]{:S(2)}) async-start(bf16[8,12,96,128]{3,2,1,0:T(8,128)(2,1)} %copy-done.3), calls=%async_computation.2 | async-start | bytes 4718592 | tf_op jit(solution)/shard_map/all_to_all | solution.py:149
  249.1 1.4 copy-start.4
Sparse Core Ops, SparseCore 0:
  60.8 36.0 all-gather.1

commit v3 on v2

--- a/solution.py
+++ b/solution.py
@@ -91,7 +91,7 @@
 
 
 def block_of(columns):
-    for block in (256, 128, 64, 32, 16):
+    for block in (384, 256, 128, 64, 32, 16):
         if columns % block == 0:
             return block
     return columns

time: 321 us -> 309 us (0.963)
  Pallas kernels: 120 us -> 108 us
    pallas_call x2, Pallas kernels: 114 us -> 102 us  [attention(): pl.pallas_call(functools.partial(attend, heads, block_of(columns)), grid=...]
  transfers between devices with their start and end apart: 3 -> 3, of which waited for: 0 -> 1; matrix products, arithmetic and copies ran while one was open for 2% -> 2% of each run, Pallas kernels for 36% -> 33%
where the time goes in v3:
time: 309 us; the launch traced here: 308 us
  blocking collectives  151 us (49%)
  Pallas kernels  108 us (35%)
  local copies, waits for them, and re-layouts  20 us (6%)
  between operations  14.2 us (5%)
  starting transfers between devices  9.69 us (3%)
  other arithmetic  4.47 us (1%)
    pallas_call x2, Pallas kernels, attention(): pl.pallas_call(functools.partial(attend, heads, block_of(columns)), grid=...  102 us
    all_to_all x1, blocking collectives, per_device(): pieces.append(lax.all_to_all(update, 'col', split_axis=0, concat_axis=0))  57.7 us
    all_to_all x1, blocking collectives, per_device(): lax.all_to_all(tiles[:, first:first + step], 'col', split_axis=0, concat_...  56.9 us
    all_to_all x1, blocking collectives, per_device(): bias_cols = lax.all_to_all(repeated, 'col', split_axis=0, concat_axis=0)  36 us
    unnamed x27, local copies, waits for them, and re-layouts  10.5 us
    pallas_call x1, Pallas kernels, normalize(): pl.pallas_call(prepare, grid=(cells // block,), in_specs=[pl.BlockSpec((b...  6.63 us
  transfers between devices with their start and end apart: 3, of which 1 were waited for; matrix products, arithmetic and copies ran while one was open for 2% of the time, Pallas kernels for 33%

profile of v3, /device:TPU:0, one launch (start us, length us, event | category | flops | bytes accessed | tf_op | source)
XLA Modules:
  0.0 308.0 jit_solution(4460429957891086356)
XLA Ops:
  7.2 0.3 broadcast_in_dim.16
  7.5 0.0 copy-start.1
  7.5 2.3 copy-done.1
  9.9 0.7 copy-done.5
  10.6 0.7 copy-done.6
  11.2 6.6 %shard_map.91 = (bf16[18432,128]{1,0:T(8,128)(2,1)S(1)}, f32[4,18432]{1,0:T(4,128)S(1)}) custom-call(bf16[18432,128]{1,0:T(8,128)(2,1)S(1)} %bitcast.13, f32[1,128]{1,0:T(1,128)S(1)} %bitcast.15, bf16[4,128]{1,0:T(4,128)(2,1)S(1)} %bitcast.14), custom_call_target="tpu_custom_call" | custom-call | tf_op jit(solution)/shard_map/pallas_call | solution.py:30
  17.8 2.2 copy-done
  20.0 0.2 reshape.37
  20.2 0.1 select_convert_fusion
  20.3 0.2 broadcast_in_dim.18
  20.4 36.0 %all_to_all.25 = bf16[8,576,128]{2,1,0:T(8,128)(2,1)S(1)} all-to-all(bf16[8,576,128]{2,1,0:T(8,128)(2,1)S(1)} %broadcast_in_dim.18), channel_id=1, replica_groups=mesh['row'=4,'col'=8] {'col'}, dimensions={0} | all-to-all | bytes 2359296 | tf_op jit(solution)/shard_map/all_to_all | solution.py:138
  56.5 1.0 reshape.38
  57.5 1.0 copy.10
  58.5 2.2 reshape.39
  60.7 0.0 all-gather.2.cloned.1.call-update
  60.7 4.7 %fusion = (bf16[8,12,96,128]{3,2,1,0:T(8,128)(2,1)S(1)}, bf16[8,12,96,128]{3,2,1,0:T(8,128)(2,1)}) fusion(bf16[8,24,96,128]{3,2,1,0:T(8,128)(2,1)} %bitcast.12), kind=kLoop, calls=%fused_computation.9 | loop fusion | bytes 9437184 | tf_op jit(solution)/shard_map/slice | solution.py:146
  65.4 56.9 %all_to_all.26.normed_ref = bf16[8,12,96,128]{3,2,1,0:T(8,128)(2,1)} all-to-all(bf16[8,12,96,128]{3,2,1,0:T(8,128)(2,1)S(1)} %get-tuple-element.9), channel_id=1, replica_groups=mesh['row'=4,'col'=8] {'col'}, dimensions={0} | all-to-all | bytes 4718592 | tf_op jit(solution)/shard_map/all_to_all | solution.py:146
  122.3 0.0 copy-start.7
  122.3 3.8 %all-to-all-start.3 = ((bf16[8,12,96,128]{3,2,1,0:T(8,128)(2,1)}), bf16[8,12,96,128]{3,2,1,0:T(8,128)(2,1)S(1)}, u32[]{:S(2)}, u32[]{:S(2)}) async-start(bf16[8,12,96,128]{3,2,1,0:T(8,128)(2,1)} %get-tuple-element.10), calls=%async_computation.3 | async-start | bytes 4718592 | tf_op jit(solution)/shard_map/all_to_all | solution.py:146
  126.1 0.1 pad_add_fusion.limits_ref
  126.3 0.0 all-gather.2.cloned.1.call-done.bias_ref
  126.3 1.7 copy-done.2
  128.0 50.8 %shard_map.92 = bf16[8,12,96,128]{3,2,1,0:T(8,128)(2,1)S(1)} custom-call(s32[2]{0:T(128)S(1)} %pad_add_fusion.limits_ref, bf16[8,12,96,128]{3,2,1,0:T(8,128)(2,1)S(1)} %copy-done.2, bf16[4,768,768]{2,1,0:T(8,128)(2,1)} %all-gather.2.cloned.1.call-done.bias_ref, bf16[128,512]{1,0:T(8,128)(2,1)S(1)} %constant_dynamic-update-slice_fusion.merged_ref, ...), custom_call_target="tpu_custom_call" | custom-call | flops 21743271936 | bytes 18874368 | tf_op jit(solution)/shard_map/pallas_call | solution.py:107
  178.8 1.5 copy-done.3
  180.3 5.9 %all-to-all-start.2 = ((bf16[8,12,96,128]{3,2,1,0:T(8,128)(2,1)}), bf16[8,12,96,128]{3,2,1,0:T(8,128)(2,1)}, u32[]{:S(2)}, u32[]{:S(2)}) async-start(bf16[8,12,96,128]{3,2,1,0:T(8,128)(2,1)} %copy-done.3), calls=%async_computation.2 | async-start | bytes 4718592 | tf_op jit(solution)/shard_map/all_to_all | solution.py:149
  186.3 0.1 pad_add_fusion.1.limits_ref
  186.3 50.9 %shard_map.93 = bf16[8,12,96,128]{3,2,1,0:T(8,128)(2,1)S(1)} custom-call(s32[2]{0:T(128)S(1)} %pad_add_fusion.1.limits_ref, bf16[8,12,96,128]{3,2,1,0:T(8,128)(2,1)S(1)} %all-to-all-done.3.normed_ref, bf16[4,768,768]{2,1,0:T(8,128)(2,1)} %all-gather.2.cloned.1.call-done.bias_ref, bf16[128,512]{1,0:T(8,128)(2,1)S(1)} %constant_dynamic-update-slice_fusion.merged_ref, ...), custom_call_target="tpu_custom_call" | custom-call | flops 21743271936 | bytes 18874368 | tf_op jit(solution)/shard_map/pallas_call | solution.py:107
  237.2 0.0 copy-start.4
  237.2 1.4 copy-done.4
  238.6 0.6 all-to-all-done.2
  239.2 57.7 %all_to_all.27 = bf16[8,12,96,128]{3,2,1,0:T(8,128)(2,1)S(1)} all-to-all(bf16[8,12,96,128]{3,2,1,0:T(8,128)(2,1)} %copy-done.4), channel_id=1, replica_groups=mesh['row'=4,'col'=8] {'col'}, dimensions={0} | all-to-all | bytes 4718592 | tf_op jit(solution)/shard_map/all_to_all | solution.py:149
  296.9 4.3 %pad_maximum_fusion = bf16[8,24,96,128]{3,2,1,0:T(8,128)(2,1)} fusion(bf16[8,12,96,128]{3,2,1,0:T(8,128)(2,1)S(1)} %all_to_all.27, bf16[8,12,96,128]{3,2,1,0:T(8,128)(2,1)} %all-to-all-done.2), kind=kLoop, calls=%fused_computation | loop fusion | flops 2359296 | bytes 9437184 | tf_op jit(solution)/shard_map/concatenate | solution.py:150
  (22 shorter events, 0.1 us)
Async XLA Ops:
  6.5 119.8 %all-gather.2.cloned.1.call-start = ((), (), s32[]{:S(2)}) async-start(), calls=%async_computation.5 | async-start | bytes 5898240 | tf_op jit(solution)/shard_map/all_gather | solution.py:141
  7.5 2.3 copy-start.1
  9.9 0.7 copy-start.5
  10.6 0.7 copy-start.6
  17.8 2.2 copy-start
  122.3 3.9 %copy-start.8 = (bf16[128,128]{1,0:T(8,128)(2,1)S(1)}, bf16[128,128]{1,0:T(8,128)(2,1)}, u32[]{:S(2)}) copy-start(bf16[128,128]{1,0:T(8,128)(2,1)} %param.11) | copy-start | bytes 98308
  122.3 3.9 %copy-start.9 = (bf16[128,128]{1,0:T(8,128)(2,1)S(1)}, bf16[128,128]{1,0:T(8,128)(2,1)}, u32[]{:S(2)}) copy-start(bf16[128,128]{1,0:T(8,128)(2,1)} %param.12) | copy-start | bytes 98308
  122.3 3.9 %copy-start.10 = (bf16[128,128]{1,0:T(8,128)(2,1)S(1)}, bf16[128,128]{1,0:T(8,128)(2,1)}, u32[]{:S(2)}) copy-start(bf16[128,128]{1,0:T(8,128)(2,1)} %param.13) | copy-start | bytes 98308
  122.3 3.9 %copy-start.11 = (bf16[128,128]{1,0:T(8,128)(2,1)S(1)}, bf16[128,128]{1,0:T(8,128)(2,1)}, u32[]{:S(2)}) copy-start(bf16[128,128]{1,0:T(8,128)(2,1)} %param.14) | copy-start | bytes 98308
  122.3 4.0 %copy-start.7 = (bf16[128,128]{1,0:T(8,128)(2,1)S(1)}, bf16[128,128]{1,0:T(8,128)(2,1)}, u32[]{:S(2)}) copy-start(bf16[128,128]{1,0:T(8,128)(2,1)} %out_w_ref.3) | copy-start | bytes 98308
  122.3 58.0 %all-to-all-start.3 = ((bf16[8,12,96,128]{3,2,1,0:T(8,128)(2,1)}), bf16[8,12,96,128]{3,2,1,0:T(8,128)(2,1)S(1)}, u32[]{:S(2)}, u32[]{:S(2)}) async-start(bf16[8,12,96,128]{3,2,1,0:T(8,128)(2,1)} %get-tuple-element.10), calls=%async_computation.3 | async-start | bytes 4718592 | tf_op jit(solution)/shard_map/all_to_all | solution.py:146
  126.3 1.7 copy-start.2
  178.8 1.5 copy-start.3
  180.3 58.9 %all-to-all-start.2 = ((bf16[8,12,96,128]{3,2,1,0:T(8,128)(2,1)}), bf16[8,12,96,128]{3,2,1,0:T(8,128)(2,1)}, u32[]{:S(2)}, u32[]{:S(2)}) async-start(bf16[8,12,96,128]{3,2,1,0:T(8,128)(2,1)} %copy-done.3), calls=%async_computation.2 | async-start | bytes 4718592 | tf_op jit(solution)/shard_map/all_to_all | solution.py:149
  237.2 1.4 copy-start.4
Sparse Core Ops, SparseCore 0:
  60.8 36.0 all-gather.1
